TPU v7x, 32 devices: a whole 2x2x4 slice. The times are simulated.
32 devices in a mesh: seq: 8 (over z, y), tp: 4 (over x, core).
Axes of the slice: x: 2, y: 2, z: 4, core: 2. Of those that a mesh axis runs over, the one named last changes fastest.
Arguments:
- query_in: bfloat16 [1024, 8192], P('seq', 'tp'), may hold values from -6 to 6
- key_in: bfloat16 [1024, 8192], P('seq', 'tp'), may hold values from -6 to 6
- value_in: bfloat16 [1024, 8192], P('seq', 'tp'), may hold values from -6 to 6
- stream: bfloat16 [1024, 8192], P('seq', 'tp'), may hold values from -6 to 6
- short_filter: float32 [3, 3, 8192], P(None, None, 'tp'), may hold values from -3 to 3
- decay_rate: float32 [16, 8192], P(None, 'tp'), as said below
- residue: float32 [16, 8192], P(None, 'tp'), as said below
- norm_gain: float32 [8192], P('tp'), may hold values from 0.5 to 1.5
- cotangent: bfloat16 [1024, 8192], P('seq', 'tp'), may hold values from -6 to 6
Outputs:
- normed: bfloat16 [1024, 8192], P('seq', 'tp')
- stream_grad: bfloat16 [1024, 8192], P('seq', 'tp')
- query_grad: bfloat16 [1024, 8192], P('seq', 'tp')
- key_grad: bfloat16 [1024, 8192], P('seq', 'tp')
- value_grad: bfloat16 [1024, 8192], P('seq', 'tp')
Inputs may be any that keep to these rules, and one draw needn't show every extreme that they name: The pole of mode m of channel c is exp(-decay_rate[m, c]); every rate is positive and at most 1/30. `residue`: residues are real numbers.
All inputs are finite; a program needn't handle non-finite values.
Results may differ from a plain program's by a relative error of at most 0.0012.
Values may be sent and summed in bfloat16 or wider, within the bound.
No kernel may reach another device: no remote copies, remote signals or barrier semaphores. Data moves between devices by JAX's collectives and lax.ppermute only.
A program may use at most 128 MiB of HBM per device.

v0:
```python
import functools

import jax
import jax.numpy as jnp
from jax import lax
from jax.experimental import pallas as pl
from jax.experimental.pallas import tpu as pltpu
from jax.sharding import PartitionSpec as P

f32 = jnp.float32
bf16 = jnp.bfloat16
epsilon = 1e-05
LANES = 128
SUB = 8
GROUP = LANES * SUB
FORWARD_EXTRA = 12
BACKWARD_EXTRA = 4
GRANT = 20 * 1024 * 1024


class Sizes:
    def __init__(self, length, channels, modes, devices):
        self.length, self.channels, self.modes, self.devices = length, channels, modes, devices
        self.tiles = channels // LANES
        self.halves = channels // GROUP
        self.direct = devices == SUB

    def chunk_row(self, r, h, extra):
        if r < self.modes:
            return h * self.modes + r
        return self.halves * self.modes + h * extra + r - self.modes

    def chunk_rows(self, extra):
        return self.halves * (self.modes + extra)

    def exchange_shape(self, extra):
        if self.direct:
            return (self.devices * self.chunk_rows(extra), LANES)
        return ((self.modes + extra) * self.tiles, LANES)

    def exchange_slice(self, r, h, extra):
        if self.direct:
            return pl.ds(self.chunk_row(r, h, extra), SUB, stride=self.chunk_rows(extra))
        return pl.ds(r * self.tiles + h * SUB, SUB)


def staged(s, block, offset, h):
    start = block * (s.tiles * SUB) + (h * SUB * SUB + offset)
    return pl.ds(start, SUB, stride=SUB)


def major(s, t, h):
    start = t * s.tiles + h * SUB
    if not isinstance(start, int):
        start = pl.multiple_of(start, SUB)
    return pl.ds(start, SUB)


def staged_before(s, block, offset, h):
    if offset < 2:
        return staged(s, block - 1, offset + SUB - 2, h)
    return staged(s, block, offset - 2, h)


def stage_rows(s, rows, out_ref, base, tiles):
    for part in range(2):
        for i, j in enumerate(tiles):
            start = base + (part * s.tiles + j) * SUB
            if not isinstance(start, int):
                start = pl.multiple_of(start, SUB)
            out_ref[pl.ds(start, SUB), :] = rows[
                part * SUB : (part + 1) * SUB, i * LANES : (i + 1) * LANES
            ]


def stage(s, x_ref, out_ref, i, h):
    start = i * 16 if isinstance(i, int) else pl.multiple_of(i * 16, 16)
    rows = x_ref[pl.ds(start, 16), h * GROUP : (h + 1) * GROUP]
    base = i * (2 * s.tiles * SUB)
    stage_rows(s, rows.astype(f32), out_ref, base, range(h * SUB, (h + 1) * SUB))


def unstage(s, in_ref, x_ref, i, h):
    base = i * (2 * s.tiles * SUB)
    row = i * 16 if isinstance(i, int) else pl.multiple_of(i * 16, 16)
    for j in range(h * SUB, (h + 1) * SUB):
        parts = []
        for part in range(2):
            start = base + (part * s.tiles + j) * SUB
            start = start if isinstance(start, int) else pl.multiple_of(start, SUB)
            parts.append(in_ref[pl.ds(start, SUB), :])
        x_ref[pl.ds(row, 16), j * LANES : (j + 1) * LANES] = jnp.concatenate(parts, axis=0).astype(bf16)


def sixteen(i, reverse=False):
    pairs = [(2 * i + part, offset) for part in range(2) for offset in range(SUB)]
    return pairs[::-1] if reverse else pairs


def stage_modes(s, x_ref, out_ref, f):
    for g in range(s.modes // SUB):
        rows = f(x_ref[g * SUB : (g + 1) * SUB, :])
        for j in range(s.tiles):
            start = (g * s.tiles + j) * SUB
            out_ref[start : start + SUB, :] = rows[:, j * LANES : (j + 1) * LANES]


def mode_tiles(s, ref, h):
    return [ref[staged(s, m // SUB, m % SUB, h), :] for m in range(s.modes)]


def stage_taps(s, filter_ref, out_ref):
    for i in range(3):
        rows = filter_ref[i]
        for j in range(s.tiles):
            start = (i * s.tiles + j) * SUB
            out_ref[start : start + 3, :] = rows[:, j * LANES : (j + 1) * LANES]


def tap_tiles(s, ref, i, h):
    return [ref[staged(s, i, tap, h), :] for tap in range(3)]


def total(parts):
    while len(parts) > 1:
        parts = [
            parts[i] + parts[i + 1] if i + 1 < len(parts) else parts[i]
            for i in range(0, len(parts), 2)
        ]
    return parts[0]


def mix(taps, now, before, before2):
    return taps[0] * now + taps[1] * before + taps[2] * before2


def begin_kernel(
    s, q_hbm, k_hbm, v_hbm, filter_hbm, decay_hbm, prod_ref, pay_ref,
    kb, vb, qb, fb, db, ks, vs, qs, taps, poles, sems,
):
    half = GROUP
    copies = [(decay_hbm, db), (filter_hbm, fb)]
    for h in range(s.halves):
        cut = pl.ds(h * half, half)
        copies += [(k_hbm.at[:, cut], kb.at[:, cut]), (v_hbm.at[:, cut], vb.at[:, cut])]
    copies.append((q_hbm.at[pl.ds(s.length - 16, 16), :], qb))
    copies = [pltpu.make_async_copy(a, b, sems.at[i]) for i, (a, b) in enumerate(copies)]
    for copy in copies:
        copy.start()
    copies[0].wait()
    stage_modes(s, db, poles, lambda x: jnp.exp(-x))
    copies[1].wait()
    stage_taps(s, fb, taps)
    blank = jnp.zeros((SUB, LANES), f32)
    steps = s.length // 16
    for h in range(s.halves):
        copies[2 + 2 * h].wait()
        copies[3 + 2 * h].wait()
        p = mode_tiles(s, poles, h)
        taps_k, taps_v = (tap_tiles(s, taps, i, h) for i in (1, 2))

        def position(block, offset, held, states, first):
            rows = staged(s, block, offset, h)
            k0, v0 = ks[rows, :], vs[rows, :]
            k1, k2, v1, v2 = held
            product = mix(taps_k, k0, k1, k2) * mix(taps_v, v0, v1, v2)
            prod_ref[major(s, block * SUB + offset, h), :] = product
            if not first:
                states = [p[m] * states[m] + product for m in range(s.modes)]
            return (k0, k1, v0, v1), states

        def bring(i):
            stage(s, kb, ks, i, h)
            stage(s, vb, vs, i, h)

        held, states = (blank,) * 4, [blank] * s.modes
        bring(0)
        for block, offset in sixteen(0):
            held, states = position(block, offset, held, states, block == 0 and offset < 2)
        bring(1)

        def step(i, carry):
            held, states = carry
            for block, offset in sixteen(i):
                held, states = position(block, offset, held, states, False)
            bring(jnp.minimum(i + 1, steps - 1))
            return held, states

        held, states = lax.fori_loop(1, steps, step, (held, states))
        for m in range(s.modes):
            pay_ref[s.exchange_slice(m, h, FORWARD_EXTRA), :] = states[m]
        if h == 0:
            copies[-1].wait()
            stage_rows(s, qb[...].astype(f32), qs, 0, range(s.tiles))
        k1, k2, v1, v2 = held
        first = [staged(s, 0, offset, h) for offset in range(2)]
        last = [staged(s, 1, offset, h) for offset in (6, 7)]
        extra = [
            ks[first[0], :], ks[first[1], :], k2, k1,
            vs[first[0], :], vs[first[1], :], v2, v1,
            qs[last[0], :], qs[last[1], :], blank, blank,
        ]
        for r, value in enumerate(extra):
            pay_ref[s.exchange_slice(s.modes + r, h, FORWARD_EXTRA), :] = value


def forward_middle(length, rates, taps, ends, extras):
    devices = len(ends)
    whole, step0, step1 = (jnp.exp(-float(length - i) * rates) for i in range(3))
    blank = jnp.zeros_like(extras[0][0])
    arriving = jnp.zeros_like(ends[0])
    result = []
    for i in range(devices):
        k0, k1, _, _, v0, v1 = extras[i][:6]
        if i:
            _, _, ka, kb, _, _, va, vb, qa, qb = extras[i - 1][:10]
        else:
            ka = kb = va = vb = qa = qb = blank
        if i + 1 < devices:
            kc, kd, _, _, vc, vd = extras[i + 1][:6]
        else:
            kc = kd = vc = vd = blank
        prod0 = mix(taps[1], k0, kb, ka) * mix(taps[2], v0, vb, va)
        prod1 = mix(taps[1], k1, k0, kb) * mix(taps[2], v1, v0, vb)
        result.append((arriving, [prod0, prod1, ka, kb, va, vb, qa, qb, kc, kd, vc, vd]))
        arriving = whole * arriving + (ends[i] + step0 * prod0 + step1 * prod1)
    return result


def backward_middle(length, rates, ends, extras):
    devices = len(ends)
    whole = jnp.exp(-float(length) * rates)
    blank = jnp.zeros_like(extras[0][0])
    arriving = jnp.zeros_like(ends[0])
    result = [None] * devices
    for i in reversed(range(devices)):
        result[i] = (arriving, extras[i + 1] if i + 1 < devices else [blank] * len(extras[0]))
        arriving = whole * arriving + ends[i]
    return result


def middle_kernel(s, extra, in_ref, decay_ref, filter_ref, out_ref):
    me = lax.axis_index("seq")
    rows = s.chunk_rows(extra)
    for h in range(s.halves):
        lanes = pl.ds(pl.multiple_of((me + h * SUB) * LANES, LANES), LANES)
        rates = decay_ref[:, lanes]
        ends, extras = [], []
        for i in range(s.devices):
            base = i * rows
            e = base + s.chunk_row(0, h, extra)
            ends.append(in_ref[e : e + s.modes, :])
            x = base + s.chunk_row(s.modes, h, extra)
            extras.append([in_ref[x + r : x + r + 1, :] for r in range(extra)])
        if extra == FORWARD_EXTRA:
            taps = [[filter_ref[i, tap : tap + 1, lanes] for tap in range(3)] for i in range(3)]
            result = forward_middle(s.length, rates, taps, ends, extras)
        else:
            result = backward_middle(s.length, rates, ends, extras)
        for i in range(s.devices):
            base = i * rows
            e = base + s.chunk_row(0, h, extra)
            out_ref[e : e + s.modes, :] = result[i][0]
            x = base + s.chunk_row(s.modes, h, extra)
            for r in range(extra):
                out_ref[x + r : x + r + 1, :] = result[i][1][r]


def exchange(s, pay, decay_rate, short_filter, extra):
    if s.direct:
        got = lax.all_to_all(pay, "seq", 0, 0, tiled=True)
        back = pl.pallas_call(
            functools.partial(middle_kernel, s, extra),
            out_shape=jax.ShapeDtypeStruct(pay.shape, f32),
            compiler_params=pltpu.CompilerParams(vmem_limit_bytes=GRANT),
        )(got, decay_rate, short_filter)
        return lax.all_to_all(back, "seq", 0, 0, tiled=True)
    rows = s.modes + extra
    width = s.channels // s.devices
    start = lax.axis_index("seq") * width
    rates = lax.dynamic_slice_in_dim(decay_rate, start, width, 1)
    part = lax.dynamic_slice_in_dim(short_filter, start, width, 2)
    pay = pay.reshape(rows, s.devices, width).transpose(1, 0, 2)
    got = lax.all_to_all(pay, "seq", 0, 0, tiled=True)
    ends = [got[i, : s.modes] for i in range(s.devices)]
    extras = [[got[i, s.modes + r][None] for r in range(extra)] for i in range(s.devices)]
    if extra == FORWARD_EXTRA:
        taps = [[part[i, tap][None] for tap in range(3)] for i in range(3)]
        result = forward_middle(s.length, rates, taps, ends, extras)
    else:
        result = backward_middle(s.length, rates, ends, extras)
    back = jnp.stack([jnp.concatenate([state] + list(more)) for state, more in result])
    back = lax.all_to_all(back, "seq", 0, 0, tiled=True)
    return back.transpose(1, 0, 2).reshape(rows * s.tiles, LANES)


def inside_kernel(s, prod_ref, decay_ref, residue_ref, inside_ref, poles, weights):
    stage_modes(s, decay_ref, poles, lambda x: jnp.exp(-x))
    stage_modes(s, residue_ref, weights, lambda x: x)
    steps = s.length // 16
    for h in range(s.halves):
        p = mode_tiles(s, poles, h)
        w = mode_tiles(s, weights, h)

        def position(block, offset, states):
            out = major(s, block * SUB + offset, h)
            product = prod_ref[out, :]
            states = [p[m] * states[m] + product for m in range(s.modes)]
            inside_ref[out, :] = total([w[m] * states[m] for m in range(s.modes)])
            return states

        states = [jnp.zeros((SUB, LANES), f32)] * s.modes
        for block, offset in sixteen(0)[2:]:
            states = position(block, offset, states)

        def step(i, states):
            for block, offset in sixteen(i):
                states = position(block, offset, states)
            return states

        lax.fori_loop(1, steps, step, states)


def forward_kernel(
    s, inside_ref, q_ref, stream_ref, cot_ref, back_ref, filter_ref, decay_ref, residue_ref, gain_ref,
    conv_ref, sums_ref,
    qs, xs, gs, taps, poles, weights, squares, inners,
):
    stage_modes(s, decay_ref, poles, lambda x: jnp.exp(-x))
    stage_modes(s, residue_ref, weights, lambda x: x)
    stage_taps(s, filter_ref, taps)

    def back(r, h):
        return back_ref[s.exchange_slice(r, h, FORWARD_EXTRA), :]

    steps = s.length // 16
    for h in range(s.halves):
        p = mode_tiles(s, poles, h)
        w = mode_tiles(s, weights, h)
        gain = gain_ref[h * SUB : (h + 1) * SUB, :]
        taps_q = tap_tiles(s, taps, 0, h)

        def position(block, offset, held, states, first):
            q1, q2 = held
            rows = staged(s, block, offset, h)
            t = block * SUB + offset
            out = major(s, t, h)
            if first:
                product = back(s.modes + offset, h)
                states = [p[m] * states[m] + product for m in range(s.modes)]
                conv = total([w[m] * states[m] for m in range(s.modes)])
                if offset == 1:
                    states = [w[m] * states[m] for m in range(s.modes)]
            else:
                states = [p[m] * states[m] for m in range(s.modes)]
                conv = inside_ref[out, :] + total(states)
            conv_ref[out, :] = conv
            q0 = qs[rows, :]
            mixed = xs[rows, :] + mix(taps_q, q0, q1, q2) * conv
            square, inner = mixed * mixed, gain * gs[rows, :] * mixed
            part = pl.ds(t * SUB if isinstance(t, int) else pl.multiple_of(t * SUB, SUB), SUB)
            if h:
                square, inner = square + squares[part, :], inner + inners[part, :]
            squares[part, :] = square
            inners[part, :] = inner
            return (q0, q1), states

        def bring(i):
            stage(s, q_ref, qs, i, h)
            stage(s, stream_ref, xs, i, h)
            stage(s, cot_ref, gs, i, h)

        held = (back(s.modes + 7, h), back(s.modes + 6, h))
        states = [back(m, h) for m in range(s.modes)]
        bring(0)
        for block, offset in sixteen(0):
            held, states = position(block, offset, held, states, block == 0 and offset < 2)
        bring(1)

        def step(i, carry):
            held, states = carry
            for block, offset in sixteen(i):
                held, states = position(block, offset, held, states, False)
            bring(jnp.minimum(i + 1, steps - 1))
            return held, states

        lax.fori_loop(1, steps, step, (held, states))
    for r, ref in enumerate((squares, inners)):
        parts = []
        for b in range(s.length // SUB):
            parts.append(
                total([ref[pl.ds(b * SUB * SUB + i, SUB, stride=SUB), :] for i in range(SUB)])
            )
        rows = jnp.concatenate(parts, axis=0)
        sums_ref[r : r + 1, :] = jnp.sum(rows.T, axis=0, keepdims=True)


def norm_kernel(
    s, width, sums_ref, conv_ref, q_ref, stream_ref, cot_ref, back_ref, filter_ref, decay_ref, gain_ref,
    normed_hbm, dstream_hbm, qgrad_hbm, dconv_ref, tail_ref, pay_ref,
    qs, xs, gs, ns, ds, normed_b, dstream_b, qgrad_b, taps, poles, inv_s, coef_s, sems,
):
    inverse = lax.rsqrt(sums_ref[0:1, :] / width + epsilon)
    coef = inverse * inverse * inverse * sums_ref[1:2, :] / width
    inv_s[...] = jnp.broadcast_to(inverse, (LANES, s.length)).T
    coef_s[...] = jnp.broadcast_to(coef, (LANES, s.length)).T
    stage_modes(s, decay_ref, poles, lambda x: jnp.exp(-x))
    stage_taps(s, filter_ref, taps)
    blocks = s.length // SUB
    blank = jnp.zeros((SUB, LANES), f32)
    copies = []

    def back(r, h):
        return back_ref[s.exchange_slice(r, h, FORWARD_EXTRA), :]

    steps = s.length // 16
    for h in range(s.halves):
        gain = gain_ref[h * SUB : (h + 1) * SUB, :]
        taps_q = tap_tiles(s, taps, 0, h)

        def position(block, offset, held, first):
            q1, q2, dq1, dq2 = held
            rows = staged(s, block, offset, h)
            t = block * SUB + offset
            out = major(s, t, h)
            inv = jnp.broadcast_to(inv_s[pl.ds(t, 1), :], (SUB, LANES))
            cf = jnp.broadcast_to(coef_s[pl.ds(t, 1), :], (SUB, LANES))
            q0 = qs[rows, :]
            qmix = mix(taps_q, q0, q1, q2)
            conv = conv_ref[out, :]
            mixed = xs[rows, :] + qmix * conv
            dmixed = inv * (gain * gs[rows, :]) - mixed * cf
            ns[rows, :] = mixed * inv * gain
            ds[rows, :] = dmixed
            dq0 = dmixed * conv
            dconv = dmixed * qmix
            dconv_ref[out, :] = dconv
            if first:
                pay_ref[s.exchange_slice(s.modes + 1 + offset, h, BACKWARD_EXTRA), :] = dq0
                if offset == 0:
                    pay_ref[s.exchange_slice(s.modes, h, BACKWARD_EXTRA), :] = dconv
            else:
                qs[staged_before(s, block, offset, h), :] = mix(taps_q, dq2, dq1, dq0)
            return q0, q1, dq0, dq1

        def bring(i):
            stage(s, q_ref, qs, i, h)
            stage(s, stream_ref, xs, i, h)
            stage(s, cot_ref, gs, i, h)

        def leave(i):
            unstage(s, ns, normed_b, i, h)
            unstage(s, ds, dstream_b, i, h)
            unstage(s, qs, qgrad_b, i, h)

        held = (back(s.modes + 7, h), back(s.modes + 6, h), blank, blank)
        bring(0)
        for block, offset in sixteen(0):
            held = position(block, offset, held, block == 0 and offset < 2)
        bring(1)

        def step(i, held):
            for block, offset in sixteen(i):
                held = position(block, offset, held, False)
            leave(i - 1)
            bring(jnp.minimum(i + 1, steps - 1))
            return held

        held = lax.fori_loop(1, steps - 1, step, held)
        for block, offset in sixteen(steps - 1):
            held = position(block, offset, held, False)
        _, _, dq1, dq2 = held
        qs[staged(s, blocks - 1, 6, h), :] = taps_q[0] * dq2 + taps_q[1] * dq1
        qs[staged(s, blocks - 1, 7, h), :] = taps_q[0] * dq1
        leave(steps - 2)
        leave(steps - 1)
        pieces = [
            (normed_b, normed_hbm, s.length),
            (dstream_b, dstream_hbm, s.length),
            (qgrad_b, qgrad_hbm, s.length - 16),
        ]
        for i, (block_ref, to_hbm, rows) in enumerate(pieces):
            cut = (pl.ds(0, rows), pl.ds(h * GROUP, GROUP))
            copy = pltpu.make_async_copy(block_ref.at[cut], to_hbm.at[cut], sems.at[3 * h + i])
            copy.start()
            copies.append(copy)
    start = (blocks - 2) * s.tiles * SUB
    tail_ref[...] = qs[start : start + 2 * s.tiles * SUB, :]
    for h in range(s.halves):
        p = mode_tiles(s, poles, h)

        def ends(i, states):
            for block, offset in sixteen(steps - 1 - i, reverse=True):
                dconv = dconv_ref[major(s, block * SUB + offset, h), :]
                states = [p[m] * states[m] + dconv for m in range(s.modes)]
            return states

        states = lax.fori_loop(0, steps, ends, [blank] * s.modes)
        for m in range(s.modes):
            pay_ref[s.exchange_slice(m, h, BACKWARD_EXTRA), :] = states[m]
        pay_ref[s.exchange_slice(s.modes + 3, h, BACKWARD_EXTRA), :] = blank
    for copy in copies:
        copy.wait()


def backward_kernel(
    s, k_ref, v_ref, dconv_ref, tail_ref, ahead_ref, back_ref, filter_ref, decay_ref, residue_ref, qgrad_in,
    qgrad_hbm, kgrad_hbm, vgrad_hbm,
    ks, vs, qs, kgrad_b, vgrad_b, qgrad_b, taps, poles, weights, sems,
):
    del qgrad_in
    stage_modes(s, decay_ref, poles, lambda x: jnp.exp(-x))
    stage_modes(s, residue_ref, weights, lambda x: x)
    stage_taps(s, filter_ref, taps)
    blocks = s.length // SUB
    copies = []

    def near(r, h):
        return ahead_ref[s.exchange_slice(s.modes + r, h, FORWARD_EXTRA), :]

    def back(r, h):
        return back_ref[s.exchange_slice(r, h, BACKWARD_EXTRA), :]

    qs[...] = tail_ref[...]
    for h in range(s.halves):
        taps_q = tap_tiles(s, taps, 0, h)
        dq0, dq1 = back(s.modes + 1, h), back(s.modes + 2, h)
        rows = [staged(s, 1, offset, h) for offset in (6, 7)]
        qs[rows[0], :] = qs[rows[0], :] + taps_q[2] * dq0
        qs[rows[1], :] = qs[rows[1], :] + (taps_q[1] * dq0 + taps_q[2] * dq1)
        unstage(s, qs, qgrad_b, 0, h)
    copy = pltpu.make_async_copy(qgrad_b, qgrad_hbm.at[pl.ds(s.length - 16, 16), :], sems.at[0])
    copy.start()
    copies.append(copy)
    steps = s.length // 16
    for h in range(s.halves):
        p = mode_tiles(s, poles, h)
        w = mode_tiles(s, weights, h)
        taps_k, taps_v = (tap_tiles(s, taps, i, h) for i in (1, 2))

        def bring(i):
            stage(s, k_ref, ks, i, h)
            stage(s, v_ref, vs, i, h)

        def leave(i):
            unstage(s, ks, kgrad_b, i, h)
            unstage(s, vs, vgrad_b, i, h)

        def advance(inputs, grads, k2, v2, d):
            k0, k1, v0, v1 = inputs
            dk1, dk2, dv1, dv2 = grads
            dk0 = d * mix(taps_v, v0, v1, v2)
            dv0 = d * mix(taps_k, k0, k1, k2)
            out = mix(taps_k, dk0, dk1, dk2), mix(taps_v, dv0, dv1, dv2)
            return (k1, k2, v1, v2), (dk0, dk1, dv0, dv1), out

        def position(block, offset, carry, before=None):
            states, inputs, grads = carry
            dconv = dconv_ref[major(s, block * SUB + offset, h), :]
            states = [p[m] * states[m] + dconv for m in range(s.modes)]
            d = total([w[m] * states[m] for m in range(s.modes)])
            if before is None:
                rows = staged_before(s, block, offset, h)
                before = ks[rows, :], vs[rows, :]
            inputs, grads, out = advance(inputs, grads, *before, d)
            rows = staged(s, block, offset, h)
            ks[rows, :], vs[rows, :] = out
            return states, inputs, grads

        bring(steps - 1)
        bring(steps - 2)
        ka, kb, va, vb, _, _, kc, kd, vc, vd = (near(2 + r, h) for r in range(10))
        arriving = [back(m, h) for m in range(s.modes)]
        dconv0 = back(s.modes, h)
        d0 = total([w[m] * arriving[m] for m in range(s.modes)])
        d1 = total([w[m] * ((arriving[m] - dconv0) / p[m]) for m in range(s.modes)])
        ends = [staged(s, blocks - 1, offset, h) for offset in (6, 7)]
        inputs = (kd, kc, vd, vc)
        grads = (jnp.zeros((SUB, LANES), f32),) * 4
        inputs, grads, _ = advance(inputs, grads, ks[ends[1], :], vs[ends[1], :], d1)
        inputs, grads, _ = advance(inputs, grads, ks[ends[0], :], vs[ends[0], :], d0)

        def step(i, carry):
            i = steps - 1 - i
            for block, offset in sixteen(i, reverse=True):
                carry = position(block, offset, carry)
            leave(i)
            bring(jnp.maximum(i - 2, 0))
            return carry

        carry = lax.fori_loop(0, steps - 1, step, (arriving, inputs, grads))
        for block, offset in sixteen(0, reverse=True):
            first = block == 0 and offset < 2
            carry = position(block, offset, carry, ((ka, va), (kb, vb))[offset] if first else None)
        leave(0)
        for i, (block_ref, to_hbm) in enumerate([(kgrad_b, kgrad_hbm), (vgrad_b, vgrad_hbm)]):
            cut = (pl.ds(0, s.length), pl.ds(h * GROUP, GROUP))
            copy = pltpu.make_async_copy(block_ref.at[cut], to_hbm.at[cut], sems.at[1 + 2 * h + i])
            copy.start()
            copies.append(copy)
    for copy in copies:
        copy.wait()


def body(
    query_in, key_in, value_in, stream, short_filter, decay_rate, residue, norm_gain, cotangent
):
    length, channels = query_in.shape
    modes = decay_rate.shape[0]
    s = Sizes(length, channels, modes, lax.axis_size("seq"))
    total_width = channels * lax.axis_size("tp")
    wide = jax.ShapeDtypeStruct((length * s.tiles, LANES), f32)
    narrow = jax.ShapeDtypeStruct((length, channels), bf16)
    rows = 16 * s.tiles
    wide_s = pltpu.VMEM(wide.shape, f32)
    narrow_s = pltpu.VMEM(narrow.shape, bf16)
    last_s = pltpu.VMEM((16, channels), bf16)
    tail_s = pltpu.VMEM((rows, LANES), f32)
    taps_s = pltpu.VMEM((3 * s.tiles * SUB, LANES), f32)
    mode_s = pltpu.VMEM((modes * s.tiles, LANES), f32)
    sum_s = pltpu.VMEM((length * SUB, LANES), f32)
    square_s = pltpu.VMEM((length, LANES), f32)
    gain = norm_gain.reshape(s.tiles, LANES)
    there = pl.BlockSpec(memory_space=pltpu.HBM)
    here = pl.BlockSpec(memory_space=pltpu.VMEM)

    def call(kernel, ins, outs, out_shape, scratch_shapes, operands, aliases={}, cost=None):
        return pl.pallas_call(
            functools.partial(kernel, s),
            in_specs=[there if c == "h" else here for c in ins],
            out_specs=[there if c == "h" else here for c in outs],
            out_shape=out_shape,
            scratch_shapes=scratch_shapes,
            input_output_aliases=aliases,
            cost_estimate=cost,
            compiler_params=pltpu.CompilerParams(vmem_limit_bytes=GRANT),
        )(*operands)

    def pay_shape(extra):
        return jax.ShapeDtypeStruct(s.exchange_shape(extra), f32)

    near_inputs = [
        pltpu.with_memory_space_constraint(x, pltpu.HBM)
        for x in (query_in, key_in, value_in, short_filter, decay_rate)
    ]
    product, pay = call(
        begin_kernel, "hhhhh", "vv",
        (wide, pay_shape(FORWARD_EXTRA)),
        [narrow_s, narrow_s, last_s, pltpu.VMEM(short_filter.shape, f32), pltpu.VMEM(decay_rate.shape, f32)]
        + [wide_s, wide_s, tail_s, taps_s, mode_s, pltpu.SemaphoreType.DMA((3 + 2 * s.halves,))],
        near_inputs,
    )
    inside = call(
        inside_kernel, "vvv", "v", (wide,), [mode_s, mode_s], (product, decay_rate, residue),
        cost=pl.CostEstimate(flops=64 * length * channels, bytes_accessed=3 * 4 * length * channels, transcendentals=0),
    )[0]
    back = exchange(s, pay, decay_rate, short_filter, FORWARD_EXTRA)
    conv, sums = call(
        forward_kernel, "v" * 9, "vv",
        (wide, jax.ShapeDtypeStruct((2, length), f32)),
        [wide_s] * 3 + [taps_s, mode_s, mode_s, sum_s, sum_s],
        (inside, query_in, stream, cotangent, back, short_filter, decay_rate, residue, gain),
    )
    sums = lax.psum(sums, "tp")
    normed, dstream, query_grad, dconv, tail, pay_back = call(
        lambda s, *refs: norm_kernel(s, total_width, *refs), "v" * 9, "hhhvvv",
        (narrow, narrow, narrow, wide, jax.ShapeDtypeStruct((rows, LANES), f32), pay_shape(BACKWARD_EXTRA)),
        [wide_s] * 5 + [narrow_s] * 3
        + [taps_s, mode_s, square_s, square_s, pltpu.SemaphoreType.DMA((3 * s.halves,))],
        (sums, conv, query_in, stream, cotangent, back, short_filter, decay_rate, gain),
    )
    back_back = exchange(s, pay_back, decay_rate, short_filter, BACKWARD_EXTRA)
    query_grad, key_grad, value_grad = call(
        backward_kernel, "v" * 9 + "h", "hhh",
        (narrow, narrow, narrow),
        [wide_s] * 2 + [tail_s] + [narrow_s] * 2 + [last_s, taps_s, mode_s, mode_s]
        + [pltpu.SemaphoreType.DMA((1 + 2 * s.halves,))],
        (key_in, value_in, dconv, tail, back, back_back, short_filter, decay_rate, residue, query_grad),
        {9: 0},
    )
    return (normed, dstream, query_grad, key_grad, value_grad)


def solution(mesh):
    cut = P("seq", "tp")
    return jax.shard_map(
        body,
        mesh=mesh,
        in_specs=(cut, cut, cut, cut, P(None, None, "tp"), P(None, "tp"), P(None, "tp"), P("tp"), cut),
        out_specs=(cut,) * 5,
        check_vma=False,
    )
```

profile of v0, /device:TPU:0, one launch (start us, length us, event | category | flops | bytes accessed | tf_op | source)
XLA Modules:
  0.0 72.4 jit_solution(15942634549952709058)
XLA Ops:
  0.6 3.3 %shard_map.128 = (f32[2048,128]{1,0:T(8,128)S(1)}, f32[448,128]{1,0:T(8,128)S(1)}) custom-call(bf16[128,2048]{1,0:T(8,128)(2,1)} %refs_2_.1, bf16[128,2048]{1,0:T(8,128)(2,1)} %k_ref.1, bf16[128,2048]{1,0:T(8,128)(2,1)} %v_ref.1, f32[3,3,2048]{2,1,0:T(4,128)} %filter_ref.7, f32[16,2048]{1,0:T(8,128)} %decay_ref.9), custom_call_target="tpu_custom_call" | custom-call | tf_op jit(solution)/shard_map/pallas_call | solution.py:628
  4.0 0.0 copy-start.8
  4.0 1.0 %copy-done.8 = f32[2048,128]{1,0:T(8,128)} copy-done((f32[2048,128]{1,0:T(8,128)}, f32[2048,128]{1,0:T(8,128)S(1)}, u32[]{:S(2)}) %copy-start.8) | copy-done | bytes 1048600
  4.9 0.0 copy-start
  4.9 0.0 copy-start.2
  4.9 15.6 %all_to_all.44 = f32[8,56,128]{2,1,0:T(8,128)S(1)} all-to-all(f32[8,56,128]{2,1,0:T(8,128)S(1)} %bitcast.16), channel_id=1, replica_groups=mesh['seq'=8,'tp'=4] {'seq'}, dimensions={0} | all-to-all | bytes 458752 | tf_op jit(solution)/shard_map/all_to_all | solution.py:271
  20.6 0.0 copy-done
  20.6 0.0 copy-done.2
  20.6 0.8 %shard_map.130 = f32[448,128]{1,0:T(8,128)} custom-call(f32[448,128]{1,0:T(8,128)S(1)} %bitcast.12, f32[16,2048]{1,0:T(8,128)S(1)} %copy-done, f32[3,3,2048]{2,1,0:T(4,128)S(1)} %copy-done.2), custom_call_target="tpu_custom_call" | custom-call | tf_op jit(solution)/shard_map/pallas_call | solution.py:272
  21.4 0.0 copy-start.7
  21.4 3.5 %all-to-all-start.1 = ((f32[8,56,128]{2,1,0:T(8,128)}), f32[8,56,128]{2,1,0:T(8,128)S(1)}, u32[]{:S(2)}, u32[]{:S(2)}) async-start(f32[8,56,128]{2,1,0:T(8,128)} %bitcast.2), calls=%async_computation.1 | async-start | bytes 458752 | tf_op jit(solution)/shard_map/all_to_all | solution.py:277
  24.9 0.0 copy-done.7
  24.9 0.0 copy-start.9
  24.9 1.2 %copy-done.9 = f32[2048,128]{1,0:T(8,128)S(1)} copy-done((f32[2048,128]{1,0:T(8,128)S(1)}, f32[2048,128]{1,0:T(8,128)}, u32[]{:S(2)}) %copy-start.9) | copy-done | bytes 1048600
  26.2 0.0 copy-start.1
  26.2 0.0 copy-start.3
  26.2 0.0 copy-start.4
  26.2 0.0 copy-start.12
  26.2 2.2 %shard_map.129.inside_ref = f32[2048,128]{1,0:T(8,128)S(1)} custom-call(f32[2048,128]{1,0:T(8,128)S(1)} %copy-done.9, f32[16,2048]{1,0:T(8,128)S(1)} %copy-done, f32[16,2048]{1,0:T(8,128)S(1)} %copy-done.7), custom_call_target="tpu_custom_call" | custom-call | flops 16777216 | bytes 3145728 | tf_op jit(solution)/shard_map/pallas_call | solution.py:628
  28.4 4.6 %all-to-all-done.1 = f32[8,56,128]{2,1,0:T(8,128)S(1)} async-done(((f32[8,56,128]{2,1,0:T(8,128)}), f32[8,56,128]{2,1,0:T(8,128)S(1)}, u32[]{:S(2)}, u32[]{:S(2)}) %all-to-all-start.1) | async-done | bytes 229408 | tf_op jit(solution)/shard_map/all_to_all | solution.py:277
  33.0 0.0 copy-done.1
  33.0 0.0 copy-done.3
  33.0 0.0 copy-done.4
  33.0 0.0 copy-done.12
  33.0 2.6 %shard_map.131 = (f32[2048,128]{1,0:T(8,128)S(1)}, f32[2,128]{1,0:T(2,128)S(1)}) custom-call(f32[2048,128]{1,0:T(8,128)S(1)} %shard_map.129.inside_ref, bf16[128,2048]{1,0:T(8,128)(2,1)S(1)} %copy-done.1, bf16[128,2048]{1,0:T(8,128)(2,1)S(1)} %copy-done.3, bf16[128,2048]{1,0:T(8,128)(2,1)S(1)} %copy-done.4, f32[448,128]{1,0:T(8,128)S(1)} %bitcast.9, ...), custom_call_target="tpu_custom_call" | custom-call | tf_op jit(solution)/shard_map/pallas_call | solution.py:628
  35.6 0.0 copy-start.10
  35.7 1.0 %copy-done.10 = f32[2048,128]{1,0:T(8,128)} copy-done((f32[2048,128]{1,0:T(8,128)}, f32[2048,128]{1,0:T(8,128)S(1)}, u32[]{:S(2)}) %copy-start.10) | copy-done | bytes 1048600
  36.6 5.6 %psum.7.refs_0_ = f32[2,128]{1,0:T(2,128)S(1)} all-reduce(f32[2,128]{1,0:T(2,128)S(1)} %get-tuple-element.20), channel_id=1, replica_groups=mesh['seq'=8,'tp'=4] {'tp'}, use_global_device_ids=true, to_apply=%region_0.0 | all-reduce | flops 256 | bytes 2048 | tf_op jit(solution)/shard_map/psum | solution.py:664
  42.3 0.0 copy-start.11
  42.3 1.2 %copy-done.11 = f32[2048,128]{1,0:T(8,128)S(1)} copy-done((f32[2048,128]{1,0:T(8,128)S(1)}, f32[2048,128]{1,0:T(8,128)}, u32[]{:S(2)}) %copy-start.11) | copy-done | bytes 1048600
  43.5 2.7 %shard_map.132 = (bf16[128,2048]{1,0:T(8,128)(2,1)}, bf16[128,2048]{1,0:T(8,128)(2,1)}, bf16[128,2048]{1,0:T(8,128)(2,1)}, f32[2048,128]{1,0:T(8,128)S(1)}, f32[...) custom-call(f32[2,128]{1,0:T(2,128)S(1)} %psum.7.refs_0_, f32[2048,128]{1,0:T(8,128)S(1)} %copy-done.11, ...), custom_call_target="tpu_custom_call" | custom-call | tf_op jit(solution)/shard_map/pallas_call | solution.py:628
  46.2 0.0 copy-start.6
  46.2 11.4 %all_to_all.45 = f32[8,40,128]{2,1,0:T(8,128)S(1)} all-to-all(f32[8,40,128]{2,1,0:T(8,128)S(1)} %bitcast.17), channel_id=1, replica_groups=mesh['seq'=8,'tp'=4] {'seq'}, dimensions={0} | all-to-all | bytes 327680 | tf_op jit(solution)/shard_map/all_to_all | solution.py:271
  57.6 0.0 copy-start.5
  57.6 10.1 %all_to_all.46 = f32[8,40,128]{2,1,0:T(8,128)S(1)} all-to-all(f32[8,40,128]{2,1,0:T(8,128)S(1)} %bitcast.14), channel_id=1, replica_groups=mesh['seq'=8,'tp'=4] {'seq'}, dimensions={0} | all-to-all | bytes 327680 | tf_op jit(solution)/shard_map/all_to_all | solution.py:277
  67.7 0.0 copy-done.6
  67.7 0.0 copy-done.5
  67.7 4.6 %shard_map.134 = (bf16[128,2048]{1,0:T(8,128)(2,1)}, bf16[128,2048]{1,0:T(8,128)(2,1)}, bf16[128,2048]{1,0:T(8,128)(2,1)}) custom-call(bf16[128,2048]{1,0:T(8,128)(2,1)S(1)} %copy-done.5, bf16[128,2048]{1,0:T(8,128)(2,1)S(1)} %copy-done.6, f32[2048,128]{1,0:T(8,128)S(1)} %get-tuple-element.24.dconv_ref, ...), custom_call_target="tpu_custom_call", output_to_operand_aliasing={{0}: (9, {})} | custom-call | tf_op jit(solution)/shard_map/pallas_call | solution.py:628
  (1 shorter events, 0.0 us)
Async XLA Ops:
  4.0 1.0 %copy-start.8 = (f32[2048,128]{1,0:T(8,128)}, f32[2048,128]{1,0:T(8,128)S(1)}, u32[]{:S(2)}) copy-start(f32[2048,128]{1,0:T(8,128)S(1)} %get-tuple-element.18.prod_ref) | copy-start | bytes 3145732
  4.9 15.6 %copy-start = (f32[16,2048]{1,0:T(8,128)S(1)}, f32[16,2048]{1,0:T(8,128)}, u32[]{:S(2)}) copy-start(f32[16,2048]{1,0:T(8,128)} %decay_ref.9) | copy-start | bytes 393220
  4.9 15.6 %copy-start.2 = (f32[3,3,2048]{2,1,0:T(4,128)S(1)}, f32[3,3,2048]{2,1,0:T(4,128)}, u32[]{:S(2)}) copy-start(f32[3,3,2048]{2,1,0:T(4,128)} %filter_ref.7) | copy-start | bytes 221188
  21.4 3.5 %copy-start.7 = (f32[16,2048]{1,0:T(8,128)S(1)}, f32[16,2048]{1,0:T(8,128)}, u32[]{:S(2)}) copy-start(f32[16,2048]{1,0:T(8,128)} %residue_ref.5) | copy-start | bytes 393220
  21.4 11.6 %all-to-all-start.1 = ((f32[8,56,128]{2,1,0:T(8,128)}), f32[8,56,128]{2,1,0:T(8,128)S(1)}, u32[]{:S(2)}, u32[]{:S(2)}) async-start(f32[8,56,128]{2,1,0:T(8,128)} %bitcast.2), calls=%async_computation.1 | async-start | bytes 458752 | tf_op jit(solution)/shard_map/all_to_all | solution.py:277
  24.9 1.2 %copy-start.9 = (f32[2048,128]{1,0:T(8,128)S(1)}, f32[2048,128]{1,0:T(8,128)}, u32[]{:S(2)}) copy-start(f32[2048,128]{1,0:T(8,128)} %copy-done.8) | copy-start | bytes 3145732
  26.2 6.9 %copy-start.1 = (bf16[128,2048]{1,0:T(8,128)(2,1)S(1)}, bf16[128,2048]{1,0:T(8,128)(2,1)}, u32[]{:S(2)}) copy-start(bf16[128,2048]{1,0:T(8,128)(2,1)} %refs_2_.1) | copy-start | bytes 1572868
  26.2 6.9 %copy-start.3 = (bf16[128,2048]{1,0:T(8,128)(2,1)S(1)}, bf16[128,2048]{1,0:T(8,128)(2,1)}, u32[]{:S(2)}) copy-start(bf16[128,2048]{1,0:T(8,128)(2,1)} %refs_3_.1) | copy-start | bytes 1572868
  26.2 6.9 %copy-start.4 = (bf16[128,2048]{1,0:T(8,128)(2,1)S(1)}, bf16[128,2048]{1,0:T(8,128)(2,1)}, u32[]{:S(2)}) copy-start(bf16[128,2048]{1,0:T(8,128)(2,1)} %refs_4_.1) | copy-start | bytes 1572868
  26.2 6.9 %copy-start.12 = (f32[2048]{0:T(1024)S(1)}, f32[2048]{0:T(1024)}, u32[]{:S(2)}) copy-start(f32[2048]{0:T(1024)} %param.16) | copy-start | bytes 24580
  35.6 1.0 %copy-start.10 = (f32[2048,128]{1,0:T(8,128)}, f32[2048,128]{1,0:T(8,128)S(1)}, u32[]{:S(2)}) copy-start(f32[2048,128]{1,0:T(8,128)S(1)} %get-tuple-element.21.refs_1_) | copy-start | bytes 3145732
  42.3 1.2 %copy-start.11 = (f32[2048,128]{1,0:T(8,128)S(1)}, f32[2048,128]{1,0:T(8,128)}, u32[]{:S(2)}) copy-start(f32[2048,128]{1,0:T(8,128)} %copy-done.10) | copy-start | bytes 3145732
  46.2 21.5 %copy-start.6 = (bf16[128,2048]{1,0:T(8,128)(2,1)S(1)}, bf16[128,2048]{1,0:T(8,128)(2,1)}, u32[]{:S(2)}) copy-start(bf16[128,2048]{1,0:T(8,128)(2,1)} %v_ref.1) | copy-start | bytes 1572868
  57.6 10.1 %copy-start.5 = (bf16[128,2048]{1,0:T(8,128)(2,1)S(1)}, bf16[128,2048]{1,0:T(8,128)(2,1)}, u32[]{:S(2)}) copy-start(bf16[128,2048]{1,0:T(8,128)(2,1)} %k_ref.1) | copy-start | bytes 1572868
where the time goes:
time: 72.8 us; the launch traced here: 72.4 us
  blocking collectives  42.7 us (59%)
  Pallas kernels  16.3 us (22%)
  waiting for transfers between devices  4.63 us (6%)
  local copies, waits for them, and re-layouts  4.42 us (6%)
  starting transfers between devices  3.53 us (5%)
  between operations  0.73 us (1%)
    all_to_all x2, blocking collectives, exchange(): got = lax.all_to_all(pay, 'seq', 0, 0, tiled=True)  27 us
    pallas_call x5, Pallas kernels, call(): pl.pallas_call(functools.partial(kernel, s), in_specs=[there if c == 'h'...  15.5 us
    all_to_all x1, blocking collectives, exchange(): return lax.all_to_all(back, 'seq', 0, 0, tiled=True)  10.1 us
    psum x1, blocking collectives, body(): sums = lax.psum(sums, 'tp')  5.63 us
    all_to_all x1, waiting for transfers between devices, exchange(): return lax.all_to_all(back, 'seq', 0, 0, tiled=True)  4.63 us
    unnamed x26, local copies, waits for them, and re-layouts  4.42 us
    all_to_all x1, starting transfers between devices, exchange(): return lax.all_to_all(back, 'seq', 0, 0, tiled=True)  3.53 us
  transfers between devices with their start and end apart: 1, of which 1 were waited for; matrix products, arithmetic and copies ran while one was open for 0% of the time, Pallas kernels for 3%

commit v1 on v0

--- a/solution.py
+++ b/solution.py
@@ -135,7 +135,7 @@
 
 
 def begin_kernel(
-    s, q_hbm, k_hbm, v_hbm, filter_hbm, decay_hbm, prod_ref, pay_ref,
+    s, q_hbm, k_hbm, v_hbm, filter_hbm, decay_hbm, pay_ref,
     kb, vb, qb, fb, db, ks, vs, qs, taps, poles, sems,
 ):
     half = GROUP
@@ -163,9 +163,8 @@
             rows = staged(s, block, offset, h)
             k0, v0 = ks[rows, :], vs[rows, :]
             k1, k2, v1, v2 = held
-            product = mix(taps_k, k0, k1, k2) * mix(taps_v, v0, v1, v2)
-            prod_ref[major(s, block * SUB + offset, h), :] = product
             if not first:
+                product = mix(taps_k, k0, k1, k2) * mix(taps_v, v0, v1, v2)
                 states = [p[m] * states[m] + product for m in range(s.modes)]
             return (k0, k1, v0, v1), states
 
@@ -294,22 +293,49 @@
     return back.transpose(1, 0, 2).reshape(rows * s.tiles, LANES)
 
 
-def inside_kernel(s, prod_ref, decay_ref, residue_ref, inside_ref, poles, weights):
-    stage_modes(s, decay_ref, poles, lambda x: jnp.exp(-x))
-    stage_modes(s, residue_ref, weights, lambda x: x)
+def inside_kernel(
+    s, k_hbm, v_hbm, filter_hbm, decay_hbm, residue_hbm, inside_ref,
+    kb, vb, fb, db, rb, ks, vs, prod, taps, poles, weights, sems,
+):
+    pairs = [(decay_hbm, db), (residue_hbm, rb), (filter_hbm, fb), (k_hbm, kb), (v_hbm, vb)]
+    copies = [pltpu.make_async_copy(a, b, sems.at[i]) for i, (a, b) in enumerate(pairs)]
+    for copy in copies:
+        copy.start()
+    for copy in copies:
+        copy.wait()
+    stage_modes(s, db, poles, lambda x: jnp.exp(-x))
+    stage_modes(s, rb, weights, lambda x: x)
+    stage_taps(s, fb, taps)
+    blank = jnp.zeros((SUB, LANES), f32)
     steps = s.length // 16
     for h in range(s.halves):
+        taps_k, taps_v = (tap_tiles(s, taps, i, h) for i in (1, 2))
+
+        def products(i, held):
+            stage(s, kb, ks, i, h)
+            stage(s, vb, vs, i, h)
+            for block, offset in sixteen(i):
+                rows = staged(s, block, offset, h)
+                k0, v0 = ks[rows, :], vs[rows, :]
+                k1, k2, v1, v2 = held
+                prod[major(s, block * SUB + offset, h), :] = (
+                    mix(taps_k, k0, k1, k2) * mix(taps_v, v0, v1, v2)
+                )
+                held = (k0, k1, v0, v1)
+            return held
+
+        lax.fori_loop(0, steps, products, (blank,) * 4)
         p = mode_tiles(s, poles, h)
         w = mode_tiles(s, weights, h)
 
         def position(block, offset, states):
             out = major(s, block * SUB + offset, h)
-            product = prod_ref[out, :]
+            product = prod[out, :]
             states = [p[m] * states[m] + product for m in range(s.modes)]
             inside_ref[out, :] = total([w[m] * states[m] for m in range(s.modes)])
             return states
 
-        states = [jnp.zeros((SUB, LANES), f32)] * s.modes
+        states = [blank] * s.modes
         for block, offset in sixteen(0)[2:]:
             states = position(block, offset, states)
 
@@ -397,8 +423,8 @@
 
 def norm_kernel(
     s, width, sums_ref, conv_ref, q_ref, stream_ref, cot_ref, back_ref, filter_ref, decay_ref, gain_ref,
-    normed_hbm, dstream_hbm, qgrad_hbm, dconv_ref, tail_ref, pay_ref,
-    qs, xs, gs, ns, ds, normed_b, dstream_b, qgrad_b, taps, poles, inv_s, coef_s, sems,
+    normed_hbm, dstream_hbm, qgrad_hbm, dconv_hbm, tail_ref, pay_ref,
+    qs, xs, gs, ns, ds, dconv_ref, normed_b, dstream_b, qgrad_b, taps, poles, inv_s, coef_s, sems,
 ):
     inverse = lax.rsqrt(sums_ref[0:1, :] / width + epsilon)
     coef = inverse * inverse * inverse * sums_ref[1:2, :] / width
@@ -484,6 +510,8 @@
             copy = pltpu.make_async_copy(block_ref.at[cut], to_hbm.at[cut], sems.at[3 * h + i])
             copy.start()
             copies.append(copy)
+    copies.append(pltpu.make_async_copy(dconv_ref, dconv_hbm, sems.at[3 * s.halves]))
+    copies[-1].start()
     start = (blocks - 2) * s.tiles * SUB
     tail_ref[...] = qs[start : start + 2 * s.tiles * SUB, :]
     for h in range(s.halves):
@@ -503,8 +531,35 @@
         copy.wait()
 
 
+def inside_back_kernel(
+    s, dconv_hbm, decay_hbm, residue_hbm, inside_ref, cs, db, rb, poles, weights, sems
+):
+    pairs = [(decay_hbm, db), (residue_hbm, rb), (dconv_hbm, cs)]
+    copies = [pltpu.make_async_copy(a, b, sems.at[i]) for i, (a, b) in enumerate(pairs)]
+    for copy in copies:
+        copy.start()
+    for copy in copies:
+        copy.wait()
+    stage_modes(s, db, poles, lambda x: jnp.exp(-x))
+    stage_modes(s, rb, weights, lambda x: x)
+    steps = s.length // 16
+    for h in range(s.halves):
+        p = mode_tiles(s, poles, h)
+        w = mode_tiles(s, weights, h)
+
+        def step(i, states):
+            for block, offset in sixteen(steps - 1 - i, reverse=True):
+                out = major(s, block * SUB + offset, h)
+                dconv = cs[out, :]
+                states = [p[m] * states[m] + dconv for m in range(s.modes)]
+                inside_ref[out, :] = total([w[m] * states[m] for m in range(s.modes)])
+            return states
+
+        lax.fori_loop(0, steps, step, [jnp.zeros((SUB, LANES), f32)] * s.modes)
+
+
 def backward_kernel(
-    s, k_ref, v_ref, dconv_ref, tail_ref, ahead_ref, back_ref, filter_ref, decay_ref, residue_ref, qgrad_in,
+    s, k_ref, v_ref, inside_ref, tail_ref, ahead_ref, back_ref, filter_ref, decay_ref, residue_ref, qgrad_in,
     qgrad_hbm, kgrad_hbm, vgrad_hbm,
     ks, vs, qs, kgrad_b, vgrad_b, qgrad_b, taps, poles, weights, sems,
 ):
@@ -556,9 +611,8 @@
 
         def position(block, offset, carry, before=None):
             states, inputs, grads = carry
-            dconv = dconv_ref[major(s, block * SUB + offset, h), :]
-            states = [p[m] * states[m] + dconv for m in range(s.modes)]
-            d = total([w[m] * states[m] for m in range(s.modes)])
+            states = [p[m] * states[m] for m in range(s.modes)]
+            d = inside_ref[major(s, block * SUB + offset, h), :] + total(states)
             if before is None:
                 rows = staged_before(s, block, offset, h)
                 before = ks[rows, :], vs[rows, :]
@@ -588,7 +642,8 @@
             bring(jnp.maximum(i - 2, 0))
             return carry
 
-        carry = lax.fori_loop(0, steps - 1, step, (arriving, inputs, grads))
+        states = [w[m] * arriving[m] for m in range(s.modes)]
+        carry = lax.fori_loop(0, steps - 1, step, (states, inputs, grads))
         for block, offset in sixteen(0, reverse=True):
             first = block == 0 and offset < 2
             carry = position(block, offset, carry, ((ka, va), (kb, vb))[offset] if first else None)
@@ -639,35 +694,51 @@
     def pay_shape(extra):
         return jax.ShapeDtypeStruct(s.exchange_shape(extra), f32)
 
-    near_inputs = [
-        pltpu.with_memory_space_constraint(x, pltpu.HBM)
-        for x in (query_in, key_in, value_in, short_filter, decay_rate)
-    ]
-    product, pay = call(
-        begin_kernel, "hhhhh", "vv",
-        (wide, pay_shape(FORWARD_EXTRA)),
-        [narrow_s, narrow_s, last_s, pltpu.VMEM(short_filter.shape, f32), pltpu.VMEM(decay_rate.shape, f32)]
+    def far(*arrays):
+        return [pltpu.with_memory_space_constraint(x, pltpu.HBM) for x in arrays]
+
+    def cost(per_element, arrays):
+        return pl.CostEstimate(
+            flops=per_element * length * channels, bytes_accessed=arrays * 4 * length * channels, transcendentals=0
+        )
+
+    filter_s = pltpu.VMEM(short_filter.shape, f32)
+    rates_s = pltpu.VMEM(decay_rate.shape, f32)
+    (pay,) = call(
+        begin_kernel, "hhhhh", "v",
+        (pay_shape(FORWARD_EXTRA),),
+        [narrow_s, narrow_s, last_s, filter_s, rates_s]
         + [wide_s, wide_s, tail_s, taps_s, mode_s, pltpu.SemaphoreType.DMA((3 + 2 * s.halves,))],
-        near_inputs,
+        far(query_in, key_in, value_in, short_filter, decay_rate),
     )
-    inside = call(
-        inside_kernel, "vvv", "v", (wide,), [mode_s, mode_s], (product, decay_rate, residue),
-        cost=pl.CostEstimate(flops=64 * length * channels, bytes_accessed=3 * 4 * length * channels, transcendentals=0),
-    )[0]
+    (inside,) = call(
+        inside_kernel, "hhhhh", "v", (wide,),
+        [narrow_s, narrow_s, filter_s, rates_s, rates_s]
+        + [wide_s] * 3 + [taps_s, mode_s, mode_s, pltpu.SemaphoreType.DMA((5,))],
+        far(key_in, value_in, short_filter, decay_rate, residue),
+        cost=cost(75, 3),
+    )
     back = exchange(s, pay, decay_rate, short_filter, FORWARD_EXTRA)
     conv, sums = call(
         forward_kernel, "v" * 9, "vv",
         (wide, jax.ShapeDtypeStruct((2, length), f32)),
         [wide_s] * 3 + [taps_s, mode_s, mode_s, sum_s, sum_s],
         (inside, query_in, stream, cotangent, back, short_filter, decay_rate, residue, gain),
+        {0: 0},
     )
     sums = lax.psum(sums, "tp")
     normed, dstream, query_grad, dconv, tail, pay_back = call(
-        lambda s, *refs: norm_kernel(s, total_width, *refs), "v" * 9, "hhhvvv",
+        lambda s, *refs: norm_kernel(s, total_width, *refs), "v" * 9, "hhhhvv",
         (narrow, narrow, narrow, wide, jax.ShapeDtypeStruct((rows, LANES), f32), pay_shape(BACKWARD_EXTRA)),
-        [wide_s] * 5 + [narrow_s] * 3
-        + [taps_s, mode_s, square_s, square_s, pltpu.SemaphoreType.DMA((3 * s.halves,))],
+        [wide_s] * 6 + [narrow_s] * 3
+        + [taps_s, mode_s, square_s, square_s, pltpu.SemaphoreType.DMA((3 * s.halves + 1,))],
         (sums, conv, query_in, stream, cotangent, back, short_filter, decay_rate, gain),
+    )
+    (inside_back,) = call(
+        inside_back_kernel, "hhh", "v", (wide,),
+        [wide_s, rates_s, rates_s, mode_s, mode_s, pltpu.SemaphoreType.DMA((3,))],
+        far(dconv, decay_rate, residue),
+        cost=cost(64, 3),
     )
     back_back = exchange(s, pay_back, decay_rate, short_filter, BACKWARD_EXTRA)
     query_grad, key_grad, value_grad = call(
@@ -675,7 +746,7 @@
         (narrow, narrow, narrow),
         [wide_s] * 2 + [tail_s] + [narrow_s] * 2 + [last_s, taps_s, mode_s, mode_s]
         + [pltpu.SemaphoreType.DMA((1 + 2 * s.halves,))],
-        (key_in, value_in, dconv, tail, back, back_back, short_filter, decay_rate, residue, query_grad),
+        (key_in, value_in, inside_back, tail, back, back_back, short_filter, decay_rate, residue, query_grad),
         {9: 0},
     )
     return (normed, dstream, query_grad, key_grad, value_grad)

time: 72.8 us -> 70.4 us (0.967)
  blocking collectives: 42.7 us -> 32.5 us
  Pallas kernels: 16.3 us -> 21.5 us
  local copies, waits for them, and re-layouts: 4.42 us -> 1.06 us
  starting transfers between devices: 3.53 us -> 6.78 us
  waiting for transfers between devices: 4.63 us -> 7.27 us
    all_to_all x1 -> x0, blocking collectives: 10.1 us -> none  [exchange(): return lax.all_to_all(back, 'seq', 0, 0, tiled=True)]
    pallas_call x5 -> x6, Pallas kernels: 15.5 us -> 19.9 us  [call(): pl.pallas_call(functools.partial(kernel, s), in_specs=[there if c == 'h'...]
    unnamed x26 -> x28, local copies, waits for them, and re-layouts: 4.42 us -> 1.06 us
    all_to_all x1 -> x2, starting transfers between devices: 3.53 us -> 6.78 us  [exchange(): return lax.all_to_all(back, 'seq', 0, 0, tiled=True)]
    all_to_all x1 -> x2, waiting for transfers between devices: 4.63 us -> 7.27 us  [exchange(): return lax.all_to_all(back, 'seq', 0, 0, tiled=True)]
  transfers between devices with their start and end apart: 1 -> 2, of which waited for: 1 -> 2; matrix products, arithmetic and copies ran while one was open for 0% -> 0% of each run, Pallas kernels for 3% -> 12%
where the time goes in v1:
time: 70.4 us; the launch traced here: 70 us
  blocking collectives  32.5 us (46%)
  Pallas kernels  21.5 us (31%)
  waiting for transfers between devices  7.27 us (10%)
  starting transfers between devices  6.78 us (10%)
  local copies, waits for them, and re-layouts  1.06 us (2%)
  between operations  0.84 us (1%)
    all_to_all x2, blocking collectives, exchange(): got = lax.all_to_all(pay, 'seq', 0, 0, tiled=True)  26.9 us
    pallas_call x6, Pallas kernels, call(): pl.pallas_call(functools.partial(kernel, s), in_specs=[there if c == 'h'...  19.9 us
    all_to_all x2, waiting for transfers between devices, exchange(): return lax.all_to_all(back, 'seq', 0, 0, tiled=True)  7.27 us
    all_to_all x2, starting transfers between devices, exchange(): return lax.all_to_all(back, 'seq', 0, 0, tiled=True)  6.78 us
    psum x1, blocking collectives, body(): sums = lax.psum(sums, 'tp')  5.67 us
    pallas_call x2, Pallas kernels, exchange(): pl.pallas_call(functools.partial(middle_kernel, s, extra), out_shape=jax....  1.51 us
  transfers between devices with their start and end apart: 2, of which 2 were waited for; matrix products, arithmetic and copies ran while one was open for 0% of the time, Pallas kernels for 12%

profile of v1, /device:TPU:0, one launch (start us, length us, event | category | flops | bytes accessed | tf_op | source)
XLA Modules:
  0.0 70.0 jit_solution(14492047351635227652)
XLA Ops:
  0.6 3.1 %shard_map.129 = f32[448,128]{1,0:T(8,128)S(1)} custom-call(bf16[128,2048]{1,0:T(8,128)(2,1)} %refs_2_.1, bf16[128,2048]{1,0:T(8,128)(2,1)} %k_ref.1, bf16[128,2048]{1,0:T(8,128)(2,1)} %v_ref.1, f32[3,3,2048]{2,1,0:T(4,128)} %filter_ref.7, f32[16,2048]{1,0:T(8,128)} %decay_ref.7), custom_call_target="tpu_custom_call" | custom-call | tf_op jit(solution)/shard_map/pallas_call | solution.py:683
  3.7 0.0 copy-start
  3.7 0.0 copy-start.3
  3.7 15.6 %all_to_all.44 = f32[8,56,128]{2,1,0:T(8,128)S(1)} all-to-all(f32[8,56,128]{2,1,0:T(8,128)S(1)} %bitcast.13), channel_id=1, replica_groups=mesh['seq'=8,'tp'=4] {'seq'}, dimensions={0} | all-to-all | bytes 458752 | tf_op jit(solution)/shard_map/all_to_all | solution.py:270
  19.4 0.0 copy-done
  19.4 0.0 copy-done.3
  19.4 0.8 %shard_map.130 = f32[448,128]{1,0:T(8,128)} custom-call(f32[448,128]{1,0:T(8,128)S(1)} %bitcast.12, f32[16,2048]{1,0:T(8,128)S(1)} %copy-done, f32[3,3,2048]{2,1,0:T(4,128)S(1)} %copy-done.3), custom_call_target="tpu_custom_call" | custom-call | tf_op jit(solution)/shard_map/pallas_call | solution.py:271
  20.2 3.4 %all-to-all-start.1 = ((f32[8,56,128]{2,1,0:T(8,128)}), f32[8,56,128]{2,1,0:T(8,128)S(1)}, u32[]{:S(2)}, u32[]{:S(2)}) async-start(f32[8,56,128]{2,1,0:T(8,128)} %bitcast.2), calls=%async_computation.1 | async-start | bytes 458752 | tf_op jit(solution)/shard_map/all_to_all | solution.py:276
  23.6 0.0 copy-start.1
  23.6 0.0 copy-start.4
  23.6 0.0 copy-start.5
  23.7 0.0 copy-start.8
  23.7 0.0 copy-start.9
  23.7 0.0 copy-start.10
  23.7 0.0 copy-start.13
  23.7 4.4 %shard_map.128.inside_ref = f32[2048,128]{1,0:T(8,128)S(1)} custom-call(bf16[128,2048]{1,0:T(8,128)(2,1)} %k_ref.1, bf16[128,2048]{1,0:T(8,128)(2,1)} %v_ref.1, f32[3,3,2048]{2,1,0:T(4,128)} %filter_ref.7, f32[16,2048]{1,0:T(8,128)} %decay_ref.7, f32[16,2048]{1,0:T(8,128)} %residue_ref.3), custom_call_target="tpu_custom_call" | custom-call | flops 19660800 | bytes 3145728 | tf_op jit(solution)/shard_map/pallas_call | solution.py:683
  28.2 3.5 %all-to-all-done.1 = f32[8,56,128]{2,1,0:T(8,128)S(1)} async-done(((f32[8,56,128]{2,1,0:T(8,128)}), f32[8,56,128]{2,1,0:T(8,128)S(1)}, u32[]{:S(2)}, u32[]{:S(2)}) %all-to-all-start.1) | async-done | bytes 229408 | tf_op jit(solution)/shard_map/all_to_all | solution.py:276
  31.7 0.0 copy-done.1
  31.7 0.0 copy-done.4
  31.7 0.0 copy-done.5
  31.7 0.0 copy-done.8
  31.7 0.0 copy-done.9
  31.7 0.0 copy-done.10
  31.7 0.0 copy-done.13
  31.8 2.2 %shard_map.131 = (f32[2048,128]{1,0:T(8,128)S(1)}, f32[2,128]{1,0:T(2,128)S(1)}) custom-call(f32[2048,128]{1,0:T(8,128)S(1)} %shard_map.128.inside_ref, bf16[128,2048]{1,0:T(8,128)(2,1)S(1)} %copy-done.5, bf16[128,2048]{1,0:T(8,128)(2,1)S(1)} %copy-done.8, bf16[128,2048]{1,0:T(8,128)(2,1)S(1)} %copy-done.9, ...), custom_call_target="tpu_custom_call", output_to_operand_aliasing={{0}: (0, {})} | custom-call | tf_op jit(solution)/shard_map/pallas_call | solution.py:683
  33.9 5.7 %psum.7.refs_0_ = f32[2,128]{1,0:T(2,128)S(1)} all-reduce(f32[2,128]{1,0:T(2,128)S(1)} %get-tuple-element.16), channel_id=1, replica_groups=mesh['seq'=8,'tp'=4] {'tp'}, use_global_device_ids=true, to_apply=%region_0.0 | all-reduce | flops 256 | bytes 2048 | tf_op jit(solution)/shard_map/psum | solution.py:729
  39.6 2.8 %shard_map.132 = (bf16[128,2048]{1,0:T(8,128)(2,1)}, bf16[128,2048]{1,0:T(8,128)(2,1)}, bf16[128,2048]{1,0:T(8,128)(2,1)}, f32[2048,128]{1,0:T(8,128)S(1)}, f32[...) custom-call(f32[2,128]{1,0:T(2,128)S(1)} %psum.7.refs_0_, f32[2048,128]{1,0:T(8,128)S(1)} %get-tuple-element.17.refs_1_, ...), custom_call_target="tpu_custom_call" | custom-call | tf_op jit(solution)/shard_map/pallas_call | solution.py:683
  42.4 0.0 copy-start.12
  42.4 1.0 %copy-done.12 = f32[2048,128]{1,0:T(8,128)} copy-done((f32[2048,128]{1,0:T(8,128)}, f32[2048,128]{1,0:T(8,128)S(1)}, u32[]{:S(2)}) %copy-start.12) | copy-done | bytes 1048600
  43.4 11.2 %all_to_all.45 = f32[8,40,128]{2,1,0:T(8,128)S(1)} all-to-all(f32[8,40,128]{2,1,0:T(8,128)S(1)} %bitcast.16), channel_id=1, replica_groups=mesh['seq'=8,'tp'=4] {'seq'}, dimensions={0} | all-to-all | bytes 327680 | tf_op jit(solution)/shard_map/all_to_all | solution.py:270
  54.6 0.7 %shard_map.134 = f32[320,128]{1,0:T(8,128)} custom-call(f32[320,128]{1,0:T(8,128)S(1)} %bitcast.14, f32[16,2048]{1,0:T(8,128)S(1)} %copy-done.1, f32[3,3,2048]{2,1,0:T(4,128)S(1)} %copy-done.4), custom_call_target="tpu_custom_call" | custom-call | tf_op jit(solution)/shard_map/pallas_call | solution.py:271
  55.3 3.4 %all-to-all-start.3 = ((f32[8,40,128]{2,1,0:T(8,128)}), f32[8,40,128]{2,1,0:T(8,128)S(1)}, u32[]{:S(2)}, u32[]{:S(2)}) async-start(f32[8,40,128]{2,1,0:T(8,128)} %bitcast.7), calls=%async_computation.3 | async-start | bytes 327680 | tf_op jit(solution)/shard_map/all_to_all | solution.py:276
  58.7 0.0 copy-start.2
  58.7 0.0 copy-start.6
  58.7 0.0 copy-start.7
  58.7 0.0 copy-start.11
  58.7 3.7 %shard_map.133.inside_ref = f32[2048,128]{1,0:T(8,128)S(1)} custom-call(f32[2048,128]{1,0:T(8,128)} %copy-done.12, f32[16,2048]{1,0:T(8,128)} %decay_ref.7, f32[16,2048]{1,0:T(8,128)} %residue_ref.3), custom_call_target="tpu_custom_call" | custom-call | flops 16777216 | bytes 3145728 | tf_op jit(solution)/shard_map/pallas_call | solution.py:683
  62.5 3.7 %all-to-all-done.3 = f32[8,40,128]{2,1,0:T(8,128)S(1)} async-done(((f32[8,40,128]{2,1,0:T(8,128)}), f32[8,40,128]{2,1,0:T(8,128)S(1)}, u32[]{:S(2)}, u32[]{:S(2)}) %all-to-all-start.3) | async-done | bytes 163872 | tf_op jit(solution)/shard_map/all_to_all | solution.py:276
  66.2 0.0 copy-done.2
  66.2 0.0 copy-done.6
  66.2 0.0 copy-done.7
  66.2 0.0 copy-done.11
  66.2 3.7 %shard_map.135 = (bf16[128,2048]{1,0:T(8,128)(2,1)}, bf16[128,2048]{1,0:T(8,128)(2,1)}, bf16[128,2048]{1,0:T(8,128)(2,1)}) custom-call(bf16[128,2048]{1,0:T(8,128)(2,1)S(1)} %copy-done.6, bf16[128,2048]{1,0:T(8,128)(2,1)S(1)} %copy-done.7, f32[2048,128]{1,0:T(8,128)S(1)} %shard_map.133.inside_ref, ...), custom_call_target="tpu_custom_call", output_to_operand_aliasing={{0}: (9, {})} | custom-call | tf_op jit(solution)/shard_map/pallas_call | solution.py:683
Async XLA Ops:
  3.7 15.7 %copy-start = (f32[16,2048]{1,0:T(8,128)S(1)}, f32[16,2048]{1,0:T(8,128)}, u32[]{:S(2)}) copy-start(f32[16,2048]{1,0:T(8,128)} %decay_ref.7) | copy-start | bytes 393220
  3.7 15.7 %copy-start.3 = (f32[3,3,2048]{2,1,0:T(4,128)S(1)}, f32[3,3,2048]{2,1,0:T(4,128)}, u32[]{:S(2)}) copy-start(f32[3,3,2048]{2,1,0:T(4,128)} %filter_ref.7) | copy-start | bytes 221188
  20.2 11.5 %all-to-all-start.1 = ((f32[8,56,128]{2,1,0:T(8,128)}), f32[8,56,128]{2,1,0:T(8,128)S(1)}, u32[]{:S(2)}, u32[]{:S(2)}) async-start(f32[8,56,128]{2,1,0:T(8,128)} %bitcast.2), calls=%async_computation.1 | async-start | bytes 458752 | tf_op jit(solution)/shard_map/all_to_all | solution.py:276
  23.6 8.1 %copy-start.1 = (f32[16,2048]{1,0:T(8,128)S(1)}, f32[16,2048]{1,0:T(8,128)}, u32[]{:S(2)}) copy-start(f32[16,2048]{1,0:T(8,128)} %decay_ref.7) | copy-start | bytes 393220
  23.6 8.1 %copy-start.4 = (f32[3,3,2048]{2,1,0:T(4,128)S(1)}, f32[3,3,2048]{2,1,0:T(4,128)}, u32[]{:S(2)}) copy-start(f32[3,3,2048]{2,1,0:T(4,128)} %filter_ref.7) | copy-start | bytes 221188
  23.6 8.1 %copy-start.5 = (bf16[128,2048]{1,0:T(8,128)(2,1)S(1)}, bf16[128,2048]{1,0:T(8,128)(2,1)}, u32[]{:S(2)}) copy-start(bf16[128,2048]{1,0:T(8,128)(2,1)} %refs_2_.1) | copy-start | bytes 1572868
  23.7 8.1 %copy-start.8 = (bf16[128,2048]{1,0:T(8,128)(2,1)S(1)}, bf16[128,2048]{1,0:T(8,128)(2,1)}, u32[]{:S(2)}) copy-start(bf16[128,2048]{1,0:T(8,128)(2,1)} %refs_3_.1) | copy-start | bytes 1572868
  23.7 8.1 %copy-start.9 = (bf16[128,2048]{1,0:T(8,128)(2,1)S(1)}, bf16[128,2048]{1,0:T(8,128)(2,1)}, u32[]{:S(2)}) copy-start(bf16[128,2048]{1,0:T(8,128)(2,1)} %refs_4_.1) | copy-start | bytes 1572868
  23.7 8.1 %copy-start.10 = (f32[16,2048]{1,0:T(8,128)S(1)}, f32[16,2048]{1,0:T(8,128)}, u32[]{:S(2)}) copy-start(f32[16,2048]{1,0:T(8,128)} %residue_ref.3) | copy-start | bytes 393220
  23.7 8.1 %copy-start.13 = (f32[2048]{0:T(1024)S(1)}, f32[2048]{0:T(1024)}, u32[]{:S(2)}) copy-start(f32[2048]{0:T(1024)} %param.16) | copy-start | bytes 24580
  42.4 1.0 %copy-start.12 = (f32[2048,128]{1,0:T(8,128)}, f32[2048,128]{1,0:T(8,128)S(1)}, u32[]{:S(2)}) copy-start(f32[2048,128]{1,0:T(8,128)S(1)} %get-tuple-element.20.dconv_hbm) | copy-start | bytes 3145732
  55.3 10.9 %all-to-all-start.3 = ((f32[8,40,128]{2,1,0:T(8,128)}), f32[8,40,128]{2,1,0:T(8,128)S(1)}, u32[]{:S(2)}, u32[]{:S(2)}) async-start(f32[8,40,128]{2,1,0:T(8,128)} %bitcast.7), calls=%async_computation.3 | async-start | bytes 327680 | tf_op jit(solution)/shard_map/all_to_all | solution.py:276
  58.7 7.5 %copy-start.2 = (f32[16,2048]{1,0:T(8,128)S(1)}, f32[16,2048]{1,0:T(8,128)}, u32[]{:S(2)}) copy-start(f32[16,2048]{1,0:T(8,128)} %decay_ref.7) | copy-start | bytes 393220
  58.7 7.5 %copy-start.6 = (bf16[128,2048]{1,0:T(8,128)(2,1)S(1)}, bf16[128,2048]{1,0:T(8,128)(2,1)}, u32[]{:S(2)}) copy-start(bf16[128,2048]{1,0:T(8,128)(2,1)} %k_ref.1) | copy-start | bytes 1572868
  58.7 7.5 %copy-start.7 = (bf16[128,2048]{1,0:T(8,128)(2,1)S(1)}, bf16[128,2048]{1,0:T(8,128)(2,1)}, u32[]{:S(2)}) copy-start(bf16[128,2048]{1,0:T(8,128)(2,1)} %v_ref.1) | copy-start | bytes 1572868
  58.7 7.5 %copy-start.11 = (f32[16,2048]{1,0:T(8,128)S(1)}, f32[16,2048]{1,0:T(8,128)}, u32[]{:S(2)}) copy-start(f32[16,2048]{1,0:T(8,128)} %residue_ref.3) | copy-start | bytes 393220
